TPU v7x, 32 devices: a whole 2x2x4 slice. The times are simulated.
32 devices in a mesh: groups: 2 (over y), dp: 4 (over z), expert: 2 (over core), cuts: 2 (over x).
Axes of the slice: x: 2, y: 2, z: 4, core: 2. Of those that a mesh axis runs over, the one named last changes fastest.
Arguments:
- tokens: bfloat16 [2048, 6144], P(('groups', 'dp', 'expert'), 'cuts'), parts along dimension 0, may hold values from -6 to 6
- routes: int32 [2048, 2], P(('groups', 'dp', 'expert')), parts along dimension 0, may hold values from 0 to 3, as said below
- gates: float32 [2048, 2], P(('groups', 'dp', 'expert')), parts along dimension 0, may hold values from 0.2 to 1
- w_gate: bfloat16 [4, 6144, 256], P('expert', None, 'cuts'), may hold values from -0.078125 to 0.078125
- w_up: bfloat16 [4, 6144, 256], P('expert', None, 'cuts'), may hold values from -0.078125 to 0.078125
- w_down: bfloat16 [4, 256, 6144], P('expert', 'cuts'), may hold values from -0.375 to 0.375
- cotangent: bfloat16 [2048, 6144], P(('groups', 'dp', 'expert'), 'cuts'), parts along dimension 0, may hold values from -0.59765625 to 0.59765625
Outputs:
- layer_out: bfloat16 [2048, 6144], P(('groups', 'dp', 'expert'), 'cuts'), parts along dimension 0
- token_grad: bfloat16 [2048, 6144], P(('groups', 'dp', 'expert'), 'cuts'), parts along dimension 0
- gate_grad: float32 [2048, 2], P(('groups', 'dp', 'expert')), parts along dimension 0
- grad_gate: float32 [8, 6144, 256], P(('groups', 'expert'), 'dp', 'cuts'), parts along dimension 0
- grad_up: float32 [8, 6144, 256], P(('groups', 'expert'), 'dp', 'cuts'), parts along dimension 0
- grad_down: float32 [8, 256, 6144], P(('groups', 'expert'), 'cuts', 'dp'), parts along dimension 0
There are 2 independent parts, one for each index of `groups`. A program takes and returns all parts, laid end to end along the dimension named above; an argument that names none is the same for every part. Nothing has to cross between parts.
Inputs may be any that keep to these rules, and one draw needn't show every extreme that they name: `routes`: A token's two experts differ. Among the 128 tokens of one block (one index pair of dp and expert), no expert is named more than 72 times, and each of the 2 experts held at the block's own index of expert is named exactly 72 times.
All inputs are finite; a program needn't handle non-finite values.
Results may differ from a plain program's by a relative error of at most 0.0073.
Values may be sent and summed in bfloat16 or wider, within the bound.
A program may use at most 128 MiB of HBM per device.

v0:
```python
import jax
import jax.numpy as jnp
from jax import lax
from jax.sharding import PartitionSpec as P

CAP = 72


def on_device(tokens, routes, gates, w_gate, w_up, w_down, cotangent):
    local_experts = w_gate.shape[0]
    experts = local_experts * lax.axis_size("expert")
    block_tokens = tokens.shape[0]
    pair_ids = routes.reshape(-1)
    onehot = (pair_ids[:, None] == jnp.arange(experts, dtype=jnp.int32)[None, :]).astype(jnp.int32)
    running = jnp.cumsum(onehot, axis=0)
    position = jnp.sum(onehot * (running - 1), axis=1)
    pair_slot = pair_ids * CAP + position
    chosen = (jnp.arange(experts * CAP, dtype=jnp.int32)[:, None] == pair_slot[None, :]).astype(
        jnp.float32
    )
    chosen = chosen.reshape(experts * CAP, block_tokens, 2)
    placed = jnp.sum(chosen, axis=2)
    slot_weight = jnp.sum(chosen * gates[None, :, :], axis=(1, 2))
    placed_bf = placed.astype(jnp.bfloat16)
    slot_x = jnp.dot(placed_bf, tokens, preferred_element_type=jnp.float32).astype(jnp.bfloat16)
    slot_cot = jnp.dot(placed_bf, cotangent, preferred_element_type=jnp.float32)
    slot_dout = (slot_weight[:, None] * slot_cot).astype(jnp.bfloat16)
    feat_cols = tokens.shape[1]
    slot_x = slot_x.reshape(experts, CAP, feat_cols)
    slot_dout = slot_dout.reshape(experts, CAP, feat_cols)
    recv_x, recv_dout = (
        lax.all_to_all(slot_x, "expert", split_axis=0, concat_axis=1, tiled=True),
        lax.all_to_all(slot_dout, "expert", split_axis=0, concat_axis=1, tiled=True),
    )
    rows_x, rows_dout = (
        lax.all_gather(recv_x, "cuts", axis=2, tiled=True),
        lax.all_gather(recv_dout, "cuts", axis=2, tiled=True),
    )
    gate_act = jnp.einsum("erd,edh->erh", rows_x, w_gate, preferred_element_type=jnp.float32)
    up_act = jnp.einsum("erd,edh->erh", rows_x, w_up, preferred_element_type=jnp.float32)
    sigma = jax.nn.sigmoid(gate_act)
    silu_act = gate_act * sigma
    hidden = (silu_act * up_act).astype(jnp.bfloat16)
    out_part = jnp.einsum("erh,ehd->erd", hidden, w_down, preferred_element_type=jnp.float32)
    d_hidden = jnp.einsum("erd,ehd->erh", rows_dout, w_down, preferred_element_type=jnp.float32)
    d_gate = (d_hidden * up_act * sigma * (1.0 + gate_act * (1.0 - sigma))).astype(jnp.bfloat16)
    d_up = (d_hidden * silu_act).astype(jnp.bfloat16)
    grad_part = jnp.einsum("erh,edh->erd", d_gate, w_gate, preferred_element_type=jnp.float32)
    grad_part = grad_part + jnp.einsum(
        "erh,edh->erd", d_up, w_up, preferred_element_type=jnp.float32
    )
    out_sum, grad_sum = (
        lax.psum_scatter(
            out_part.astype(jnp.bfloat16), "cuts", scatter_dimension=2, tiled=True
        ).astype(jnp.float32),
        lax.psum_scatter(
            grad_part.astype(jnp.bfloat16), "cuts", scatter_dimension=2, tiled=True
        ).astype(jnp.float32),
    )
    back_out, back_grad = (
        lax.all_to_all(
            out_sum.astype(jnp.bfloat16), "expert", split_axis=1, concat_axis=0, tiled=True
        ),
        lax.all_to_all(
            grad_sum.astype(jnp.bfloat16), "expert", split_axis=1, concat_axis=0, tiled=True
        ),
    )
    out_flat = back_out.reshape(experts * CAP, feat_cols)
    grad_flat = back_grad.reshape(experts * CAP, feat_cols)
    first_out = jnp.dot(
        chosen[:, :, 0].T.astype(jnp.bfloat16), out_flat, preferred_element_type=jnp.float32
    )
    second_out = jnp.dot(
        chosen[:, :, 1].T.astype(jnp.bfloat16), out_flat, preferred_element_type=jnp.float32
    )
    layer_out = (gates[:, 0:1] * first_out + gates[:, 1:2] * second_out).astype(jnp.bfloat16)
    token_grad = jnp.dot(placed_bf.T, grad_flat, preferred_element_type=jnp.float32).astype(
        jnp.bfloat16
    )
    scores = jnp.einsum("sd,td->st", out_flat, cotangent, preferred_element_type=jnp.float32)
    gate_part = jnp.sum(chosen * scores[:, :, None], axis=0)
    gate_grad = lax.psum(gate_part, "cuts")
    cols_x, cols_dout = (
        lax.all_to_all(rows_x, "dp", split_axis=2, concat_axis=1, tiled=True),
        lax.all_to_all(rows_dout, "dp", split_axis=2, concat_axis=1, tiled=True),
    )
    part_hidden = lax.all_gather(hidden, "dp", axis=1, tiled=True)
    part_gate = lax.all_gather(d_gate, "dp", axis=1, tiled=True)
    part_up = lax.all_gather(d_up, "dp", axis=1, tiled=True)
    grad_g = jnp.einsum("erd,erh->edh", cols_x, part_gate, preferred_element_type=jnp.float32)
    grad_u = jnp.einsum("erd,erh->edh", cols_x, part_up, preferred_element_type=jnp.float32)
    grad_d = jnp.einsum("erh,erd->ehd", part_hidden, cols_dout, preferred_element_type=jnp.float32)
    return (layer_out, token_grad, gate_grad, grad_g, grad_u, grad_d)


def solution(mesh):
    in_specs = (
        P(("groups", "dp", "expert"), "cuts"),
        P(("groups", "dp", "expert"), None),
        P(("groups", "dp", "expert"), None),
        P("expert", None, "cuts"),
        P("expert", None, "cuts"),
        P("expert", "cuts", None),
        P(("groups", "dp", "expert"), "cuts"),
    )
    out_specs = (
        P(("groups", "dp", "expert"), "cuts"),
        P(("groups", "dp", "expert"), "cuts"),
        P(("groups", "dp", "expert"), None),
        P(("groups", "expert"), "dp", "cuts"),
        P(("groups", "expert"), "dp", "cuts"),
        P(("groups", "expert"), "cuts", "dp"),
    )
    return jax.shard_map(
        on_device, mesh=mesh, in_specs=in_specs, out_specs=out_specs, check_vma=False
    )
```

profile of v0, /device:TPU:0, one launch (start us, length us, event | category | flops | bytes accessed | tf_op | source)
XLA Modules:
  0.0 551.4 jit_solution(13992056372430463501)
XLA Ops:
  12.8 5.2 all_to_all.102
  19.4 52.2 %all-gather.3.cloned.1.call-done = bf16[2,144,6144]{2,1,0:T(8,128)(2,1)} async-done(((bf16[2,144,3072]{2,1,0:T(8,128)(2,1)}), bf16[2,144,6144]{2,1,0:T(8,128)(2,1)}) %all-gather.3.cloned.1.call-update) | async-done | bytes 3538960 | tf_op jit(solution)/shard_map/all_gather | solution.py:36
  71.5 4.2 fusion.10
  81.1 47.8 %reduce-scatter.3.cloned.1.call-done = bf16[2,144,3072]{2,1,0:T(8,128)(2,1)} async-done(((bf16[2,144,6144]{2,1,0:T(8,128)(2,1)}), bf16[2,144,3072]{2,1,0:T(8,128)(2,1)}) %reduce-scatter.3.cloned.1.call-update) | async-done | bytes 1769488 | tf_op jit(solution)/shard_map/reduce_scatter | solution.py:53
  128.9 3.3 copy.74
  132.2 5.2 all_to_all.103
  139.9 5.2 all_to_all.104
  146.5 15.8 %copy.81 = bf16[2,144,6144]{1,0,2:T(2,128)(2,1)} copy(bf16[2,144,6144]{2,1,0:T(8,128)(2,1)} %all-gather.3.cloned.1.call-done) | data formatting | bytes 7077888 | tf_op jit(solution)/shard_map/all_gather | solution.py:36
  162.3 5.2 all-to-all-start.4
  167.8 28.2 %all-gather.5.cloned.1.call-done = bf16[2,144,6144]{2,1,0:T(8,128)(2,1)} async-done(((bf16[2,144,3072]{2,1,0:T(8,128)(2,1)}), bf16[2,144,6144]{2,1,0:T(8,128)(2,1)}) %all-gather.5.cloned.1.call-update) | async-done | bytes 3538960 | tf_op jit(solution)/shard_map/all_gather | solution.py:37
  196.0 3.2 multiply_convert_fusion
  201.2 3.0 fusion
  204.2 15.7 %copy.83 = bf16[2,144,6144]{1,0,2:T(2,128)(2,1)} copy(bf16[2,144,6144]{2,1,0:T(8,128)(2,1)} %all-gather.5.cloned.1.call-done) | data formatting | bytes 7077888 | tf_op jit(solution)/shard_map/all_gather | solution.py:37
  219.9 86.3 %all-to-all-done.4 = bf16[2,144,6144]{1,0,2:T(2,128)(2,1)} async-done(((bf16[2,144,6144]{1,0,2:T(2,128)(2,1)}), bf16[2,144,6144]{1,0,2:T(2,128)(2,1)}, u32[]{:S(2)}, u32[]{:S(2)}) %all-to-all-start.4) | async-done | bytes 3538976 | tf_op jit(solution)/shard_map/all_to_all | solution.py:84
  306.2 5.2 all-to-all-start.5
  311.5 145.8 %all_gather.19 = bf16[2,576,128]{2,1,0:T(8,128)(2,1)S(1)} all-gather(bf16[2,144,128]{2,1,0:T(8,128)(2,1)S(1)} %get-tuple-element.12), channel_id=1, replica_groups=mesh['groups'=2,'dp'=4,'expert'=2,'cuts'=2] {'dp'}, dimensions={1}, use_global_device_ids=true | all-gather | bytes 368640 | tf_op jit(solution)/shard_map/all_gather | solution.py:87
  457.3 15.9 %copy.82 = bf16[2,144,4,1536]{3,1,2,0:T(8,128)(2,1)} copy(bf16[2,144,4,1536]{1,0,3,2:T(2,128)(2,1)} %bitcast.20) | data formatting | bytes 7077888 | tf_op jit(solution)/shard_map/all_to_all | solution.py:84
  473.2 5.5 psum.7
  480.8 14.3 %all_gather.18 = bf16[2,576,128]{2,1,0:T(8,128)(2,1)S(1)} all-gather(bf16[2,144,128]{2,1,0:T(8,128)(2,1)S(1)} %get-tuple-element.8), channel_id=1, replica_groups=mesh['groups'=2,'dp'=4,'expert'=2,'cuts'=2] {'dp'}, dimensions={1}, use_global_device_ids=true | all-gather | bytes 368640 | tf_op jit(solution)/shard_map/all_gather | solution.py:89
  495.1 14.0 %all_gather.17 = bf16[2,576,128]{2,1,0:T(8,128)(2,1)S(1)} all-gather(bf16[2,144,128]{2,1,0:T(8,128)(2,1)S(1)} %copy-done.11), channel_id=1, replica_groups=mesh['groups'=2,'dp'=4,'expert'=2,'cuts'=2] {'dp'}, dimensions={1}, use_global_device_ids=true | all-gather | bytes 368640 | tf_op jit(solution)/shard_map/all_gather | solution.py:88
  514.7 15.7 %copy.84 = bf16[2,144,4,1536]{3,1,2,0:T(8,128)(2,1)} copy(bf16[2,144,4,1536]{1,0,3,2:T(2,128)(2,1)} %bitcast.24) | data formatting | bytes 7077888 | tf_op jit(solution)/shard_map/all_to_all | solution.py:85
  530.4 4.0 fusion.15
  534.4 3.3 copy.78
  537.6 5.2 all_to_all.105
  (72 shorter events, 28.1 us)
Async XLA Ops:
  7.2 71.0 %copy-start = (bf16[2,128,6144]{2,1,0:T(8,128)(2,1)S(1)}, bf16[2,128,6144]{2,1,0:T(8,128)(2,1)}, u32[]{:S(2)}) copy-start(bf16[2,128,6144]{2,1,0:T(8,128)(2,1)} %param.12) | copy-start | bytes 9437188
  7.2 64.3 %all-gather.3.cloned.1.call-start = ((), (), s32[]{:S(2)}) async-start(), calls=%async_computation.8 | async-start | bytes 5308416 | tf_op jit(solution)/shard_map/all_gather | solution.py:36
  19.3 109.6 %reduce-scatter.3.cloned.1.call-start = ((), (), s32[]{:S(2)}) async-start(), calls=%async_computation.9 | async-start | bytes 5308416 | tf_op jit(solution)/shard_map/reduce_scatter | solution.py:53
  71.5 4.2 copy-start.4
  71.5 4.9 copy-start.6
  81.1 114.9 %all-gather.5.cloned.1.call-start = ((), (), s32[]{:S(2)}) async-start(), calls=%async_computation.10 | async-start | bytes 5308416 | tf_op jit(solution)/shard_map/all_gather | solution.py:37
  137.4 1.1 copy-start.9
  137.8 1.4 copy-start.12
  137.9 2.0 copy-start.2
  162.3 144.0 %all-to-all-start.4 = ((bf16[2,144,6144]{1,0,2:T(2,128)(2,1)}), bf16[2,144,6144]{1,0,2:T(2,128)(2,1)}, u32[]{:S(2)}, u32[]{:S(2)}) async-start(bf16[2,144,6144]{1,0,2:T(2,128)(2,1)} %copy.81), calls=%async_computation.6 | async-start | bytes 12582912 | tf_op jit(solution)/shard_map/all_to_all | solution.py:84
  167.5 366.8 %reduce-scatter.5.cloned.1.call-start = ((), (), s32[]{:S(2)}) async-start(), calls=%async_computation.11 | async-start | bytes 5308416 | tf_op jit(solution)/shard_map/reduce_scatter | solution.py:56
  196.0 3.3 copy-start.8
  199.3 1.1 copy-start.10
  199.3 1.9 copy-start.7
  306.2 208.4 %all-to-all-start.5 = ((bf16[2,144,6144]{1,0,2:T(2,128)(2,1)}), bf16[2,144,6144]{1,0,2:T(2,128)(2,1)}, u32[]{:S(2)}, u32[]{:S(2)}) async-start(bf16[2,144,6144]{1,0,2:T(2,128)(2,1)} %copy.83), calls=%async_computation.7 | async-start | bytes 12582912 | tf_op jit(solution)/shard_map/all_to_all | solution.py:85
  457.3 21.4 %copy-start.3 = (bf16[2,2,72,3072]{3,2,1,0:T(8,128)(2,1)S(1)}, bf16[2,2,72,3072]{3,2,1,0:T(8,128)(2,1)}, u32[]{:S(2)}) copy-start(bf16[2,2,72,3072]{3,2,1,0:T(8,128)(2,1)} %copy-done.2) | copy-start | bytes 5308420
  478.7 16.4 %copy-start.11 = (bf16[2,144,128]{2,1,0:T(8,128)(2,1)S(1)}, bf16[2,144,128]{2,1,0:T(8,128)(2,1)}, u32[]{:S(2)}) copy-start(bf16[2,144,128]{2,1,0:T(8,128)(2,1)} %copy-done.10) | copy-start | bytes 221188
  479.3 29.8 %copy-start.5 = (bf16[2,144,4,1536]{3,1,2,0:T(8,128)(2,1)S(1)}, bf16[2,144,4,1536]{3,1,2,0:T(8,128)(2,1)}, u32[]{:S(2)}) copy-start(bf16[2,144,4,1536]{3,1,2,0:T(8,128)(2,1)} %copy.82) | copy-start | bytes 10616836
  542.8 2.0 copy-start.1
Sparse Core Ops, SparseCore 0:
  19.4 52.0 all-gather.2
  81.2 47.6 reduce-scatter.2
  146.6 49.3 all-gather.4
  204.3 47.6 reduce-scatter.4
where the time goes:
time: 554 us; the launch traced here: 551 us
  waiting for transfers between devices  215 us (39%)
  blocking collectives  200 us (36%)
  local copies, waits for them, and re-layouts  77.3 us (14%)
  matrix products  32.2 us (6%)
  between operations  14 us (3%)
  starting transfers between devices  10.8 us (2%)
    all_gather x1, blocking collectives, on_device(): part_hidden = lax.all_gather(hidden, 'dp', axis=1, tiled=True)  146 us
    all_to_all x1, waiting for transfers between devices, on_device(): lax.all_to_all(rows_x, 'dp', split_axis=2, concat_axis=1, tiled=True)  86.3 us
    all_gather x1, waiting for transfers between devices, on_device(): lax.all_gather(recv_x, 'cuts', axis=2, tiled=True)  52.2 us
    reduce_scatter x1, waiting for transfers between devices, on_device(): lax.psum_scatter(out_part.astype(jnp.bfloat16), 'cuts', scatter_dimension...  47.8 us
    all_gather x1, waiting for transfers between devices, on_device(): lax.all_gather(recv_dout, 'cuts', axis=2, tiled=True)  28.2 us
    all_to_all x1, local copies, waits for them, and re-layouts, on_device(): lax.all_to_all(rows_x, 'dp', split_axis=2, concat_axis=1, tiled=True)  15.9 us
    all_gather x1, local copies, waits for them, and re-layouts, on_device(): lax.all_gather(recv_x, 'cuts', axis=2, tiled=True)  15.8 us
    all_to_all x1, local copies, waits for them, and re-layouts, on_device(): lax.all_to_all(rows_dout, 'dp', split_axis=2, concat_axis=1, tiled=True)  15.7 us
  transfers between devices with their start and end apart: 6, of which 4 were waited for; matrix products, arithmetic and copies ran while one was open for 15% of the time, Pallas kernels for 0%

commit v1 on v0

v1 whole, which is shorter than its diff:
```python
import functools

import jax
import jax.numpy as jnp
from jax import lax
from jax.experimental import pallas as pl
from jax.experimental.pallas import tpu as pltpu
from jax.sharding import PartitionSpec as P

MESH = pl.DeviceIdType.MESH
BF = jnp.bfloat16
F32 = jnp.float32


def dot(a, b, ca, cb):
    return lax.dot_general(a, b, (((ca,), (cb,)), ((), ())), preferred_element_type=F32)


def tile_of(width):
    for tile in (512, 384, 256, 128):
        if width % tile == 0:
            return tile
    return width


def kernel(
    N, C, tok, cot, aux_own, aux_oth, wg, wu, wd_in,
    out_o, grad_o, gg_o, g_gate, g_up, g_down,
    wgu, wd, xg, zr, hz, aux, acc, accd, hid, ploc, csend, cr, xsend, xr, ggs, ggr, hwt,
    wsem, osem, xs_s, xs_r, co_s, co_r, au_s, au_r, z_s, z_r, zl, f_s, f_r,
    h_s, h_r, rc_s, rc_r, rx_s, rx_r, gg_s, gg_r,
):
    d, e, c = lax.axis_index("dp"), lax.axis_index("expert"), lax.axis_index("cuts")
    other = 1 - e
    rows = tok.shape[0]
    R = N // C
    Dq = tok.shape[1] // R
    ins = (tok, cot)
    K = wg.shape[0]
    W = wg.shape[2]

    def rel(i):
        return lax.rem(c + i, C)

    def quarter(p):
        return rel(p // R) * R + p % R

    def cols(p):
        return pl.ds(pl.multiple_of(quarter(p) * Dq, 128), Dq)

    def rcopy(src, dst, ss, rs, dev):
        return pltpu.make_async_remote_copy(
            src_ref=src, dst_ref=dst, send_sem=ss, recv_sem=rs, device_id=dev, device_id_type=MESH
        )

    barrier = pltpu.get_barrier_semaphore()
    peers = [{"cuts": rel(i)} for i in range(1, C)]
    peers += [{"expert": other, "cuts": rel(i)} for i in range(C)]
    peers += [{"dp": lax.rem(d + i, N)} for i in range(1, N)]
    for peer in peers:
        pl.semaphore_signal(barrier, inc=1, device_id=peer, device_id_type=MESH)
    pl.semaphore_wait(barrier, len(peers))

    own = pl.ds(0, rows)
    oth = pl.ds(rows, rows)
    core = {"expert": other}

    x_out = []
    c_out = []
    loc = []
    aux_copy = rcopy(aux_oth, aux.at[1], au_s, au_r, core)
    aux_copy.start()
    aux_loc = pltpu.make_async_copy(aux_own, aux.at[0], wsem.at[2 * K + 1])
    aux_loc.start()
    for kind in range(2):
        for r in range(R):
            src = ins[kind].at[:, pl.ds(r * Dq, Dq)]
            for i in range(1, C):
                p = (C - i) * R + r
                cp = rcopy(src, xg.at[kind, p, own], xs_s.at[kind, p], xs_r.at[kind, p], {"cuts": rel(i)})
                cp.start()
                x_out.append(cp)
            cp = rcopy(src, xg.at[kind, r, oth], co_s.at[kind, r], co_r.at[kind, r], core)
            cp.start()
            c_out.append(cp)
            cp = pltpu.make_async_copy(src, xg.at[kind, r, own], osem.at[kind, r])
            cp.start()
            loc.append(cp)
    w_loads = []
    for k in range(K):
        for j, w in enumerate((wg, wu)):
            cp = pltpu.make_async_copy(
                w.at[k], wgu.at[:, pl.ds((2 * k + j) * W, W)], wsem.at[2 * k + j]
            )
            cp.start()
            w_loads.append(cp)
    wd_load = pltpu.make_async_copy(wd_in, wd, wsem.at[2 * K])
    wd_load.start()

    def z_copy(kind, p):
        q = quarter(p)
        return rcopy(
            xg.at[kind, p, own], zr.at[kind, d, own], z_s.at[kind, p], z_r.at[kind, d], {"dp": q}
        )

    def z_local(kind, p):
        return pltpu.make_async_copy(xg.at[kind, p], zr.at[kind, d], zl.at[kind])

    def arrive(kind, p):
        if p < R:
            loc[kind * R + p].wait()
        else:
            rcopy(
                xg.at[kind, p, own], xg.at[kind, p, own], xs_s.at[kind, p], xs_r.at[kind, p],
                {"cuts": c},
            ).wait_recv()
            cp = rcopy(
                xg.at[kind, p, own], xg.at[kind, p, oth], co_s.at[kind, p], co_r.at[kind, p], core
            )
            cp.start()
            c_out.append(cp)

        @pl.when(quarter(p) != d)
        def _():
            z_copy(kind, p).start()

        rcopy(
            xg.at[kind, p, own], xg.at[kind, p, oth], co_s.at[kind, p], co_r.at[kind, p], core
        ).wait_recv()

        @pl.when(quarter(p) == d)
        def _():
            z_local(kind, p).start()

    acc[...] = jnp.zeros_like(acc)
    accd[...] = jnp.zeros_like(accd)
    for cp in w_loads:
        cp.wait()
    for p in range(N):
        arrive(0, p)
        acc[...] += dot(xg[0, p], wgu[cols(p), :], 1, 0)
    aux_copy.wait()
    aux_loc.wait()
    wd_load.wait()

    def weight(k):
        return jnp.concatenate([aux[0, :, k : k + 1], aux[1, :, k : k + 1]], axis=0)

    for k in range(K):
        gs = pl.ds(2 * k * W, W)
        us = pl.ds((2 * k + 1) * W, W)
        g = acc[:, gs]
        u = acc[:, us]
        s = jax.nn.sigmoid(g)
        silu = g * s
        h = silu * u
        w = weight(k)
        hid[:, pl.ds(k * W, W)] = h
        hz[d, :, pl.ds((2 * K + k) * W, W)] = (h * w).astype(BF)
        acc[:, gs] = u * s * (1.0 + g * (1.0 - s)) * w
        acc[:, us] = silu * w

    tile = tile_of(Dq)
    rx_out = []
    rc_out = []

    def back(kind):
        order = list(range(R, N)) + list(range(R))
        for p in order:
            base = quarter(p) * Dq

            def step(t, _, p=p, base=base):
                at = pl.ds(pl.multiple_of(t * tile, 128), tile)
                wat = pl.ds(pl.multiple_of(base + t * tile, 128), tile)
                if kind == 0:
                    part = dot(hz[d, :, pl.ds(2 * K * W, K * W)], wd[:, wat], 1, 0)
                else:
                    part = dot(hz[d, :, pl.ds(0, 2 * K * W)], wgu[wat, :], 1, 1)
                ploc[kind, p, :, at] = part[:rows]
                csend[kind, p, :, at] = part[rows:].astype(BF)
                return 0

            lax.fori_loop(0, Dq // tile, step, 0)
            cp = rcopy(csend.at[kind, p], cr.at[kind, p], rc_s.at[kind, p], rc_r.at[kind, p], core)
            cp.start()
            rc_out.append(cp)
        for p in order[: N - R]:
            rcopy(
                csend.at[kind, p], cr.at[kind, p], rc_s.at[kind, p], rc_r.at[kind, p], core
            ).wait_recv()
            xsend[kind, p - R] = (ploc[kind, p] + cr[kind, p].astype(F32)).astype(BF)
            cp = rcopy(
                xsend.at[kind, p - R], xr.at[kind, p - R], rx_s.at[kind, p - R],
                rx_r.at[kind, p - R], {"cuts": rel(p // R)},
            )
            cp.start()
            rx_out.append(cp)

    back(0)

    for p in range(N):
        arrive(1, p)
        accd[...] += dot(xg[1, p], wd[:, cols(p)], 1, 1)

    ggs[...] = jnp.zeros_like(ggs)
    for k in range(K):
        dh = accd[:, pl.ds(k * W, W)]
        prod = hid[:, pl.ds(k * W, W)] * dh
        for slot in range(2):
            piece = prod[slot * rows : (slot + 1) * rows]
            ggs[slot, pl.ds(k, 1), :] = jnp.sum(piece.T, axis=0, keepdims=True)
        hz[d, :, pl.ds(2 * k * W, W)] = (acc[:, pl.ds(2 * k * W, W)] * dh).astype(BF)
        hz[d, :, pl.ds((2 * k + 1) * W, W)] = (acc[:, pl.ds((2 * k + 1) * W, W)] * dh).astype(BF)

    gg_out = []
    for i in range(C):
        for slot in range(2):
            if i == 0 and slot == 0:
                continue
            dev = {"cuts": rel(i)} if slot == 0 else {"expert": other, "cuts": rel(i)}
            cp = rcopy(ggs.at[slot], ggr.at[slot, i], gg_s.at[slot, i], gg_r.at[slot, i], dev)
            cp.start()
            gg_out.append(cp)
    ggr[0, 0] = ggs[0]

    h_out = []
    for i in range(1, N):
        cp = rcopy(hz.at[d], hz.at[d], h_s.at[i], h_r.at[d], {"dp": lax.rem(d + i, N)})
        cp.start()
        h_out.append(cp)

    back(1)

    f_out = []
    for kind in range(2):
        for i in range(1, N):
            ds = lax.rem(d + i, N)
            z = zr.at[kind, ds, own]
            rcopy(z, z, z_s.at[kind, i], z_r.at[kind, ds], {"dp": d}).wait_recv()
            cp = rcopy(z, zr.at[kind, ds, oth], f_s.at[kind, ds], f_r.at[kind, ds], core)
            cp.start()
            f_out.append(cp)
    for i in range(1, N):
        ds = lax.rem(d + i, N)
        rcopy(hz.at[ds], hz.at[ds], h_s.at[i], h_r.at[ds], {"dp": d}).wait_recv()
    for kind in range(2):
        z_local(kind, 0).wait()
        for i in range(1, N):
            ds = lax.rem(d + i, N)
            z = zr.at[kind, ds, oth]
            rcopy(z, z, f_s.at[kind, ds], f_r.at[kind, ds], core).wait_recv()

    flat = N * 2 * rows
    hwt[...] = hz[:, :, pl.ds(2 * K * W, K * W)].reshape(flat, K * W).T
    wt = 256 if Dq % 256 == 0 else 128

    def wstep(t, _):
        at = pl.ds(pl.multiple_of(t * wt, 128), wt)
        full = dot(
            zr[0, :, :, at].reshape(flat, wt), hz[:, :, pl.ds(0, 2 * K * W)].reshape(flat, 2 * K * W), 0, 0
        )
        down = dot(hwt[...], zr[1, :, :, at].reshape(flat, wt), 1, 0)
        for k in range(K):
            g_gate[k, at, :] = full[:, 2 * k * W : (2 * k + 1) * W]
            g_up[k, at, :] = full[:, (2 * k + 1) * W : (2 * k + 2) * W]
            g_down[k, :, at] = down[k * W : (k + 1) * W]
        return 0

    lax.fori_loop(0, Dq // wt, wstep, 0)

    outs = (out_o, grad_o)
    for kind in range(2):
        for r in range(R):
            rcopy(
                csend.at[kind, r], cr.at[kind, r], rc_s.at[kind, r], rc_r.at[kind, r], core
            ).wait_recv()
            total = ploc[kind, r] + cr[kind, r].astype(F32)
            for i in range(1, C):
                n = (i - 1) * R + r
                rcopy(
                    xr.at[kind, n], xr.at[kind, n], rx_s.at[kind, n], rx_r.at[kind, n], {"cuts": c}
                ).wait_recv()
                total = total + xr[kind, n].astype(F32)
            outs[kind][:, pl.ds(r * Dq, Dq)] = total.astype(BF)

    for i in range(C):
        for slot in range(2):
            if i or slot:
                g = ggr.at[slot, i]
                rcopy(g, g, gg_s.at[slot, i], gg_r.at[slot, i], {"cuts": c}).wait_recv()
    gg_o[...] = jnp.sum(ggr[...], axis=1)

    for cp in x_out + c_out + rc_out + rx_out + gg_out + h_out + f_out:
        cp.wait_send()
    for kind in range(2):
        for p in range(N):
            @pl.when(quarter(p) != d)
            def _():
                z_copy(kind, p).wait_send()


def on_device(N, C, tokens, routes, gates, w_gate, w_up, w_down, cotangent):
    K, D, W = w_gate.shape
    rows, Dc = tokens.shape
    R = N // C
    Dq = Dc // R
    e = lax.axis_index("expert")
    lanes = jnp.arange(128, dtype=jnp.int32)
    onehot = (routes[:, :, None] == lanes[None, None, :]) & (lanes < 2 * K)[None, None, :]
    dense = jnp.sum(jnp.where(onehot, gates[:, :, None], 0.0), axis=1)
    low, high = dense, jnp.roll(dense, -K, axis=1)
    aux_own = jnp.where(e == 0, low, high)
    aux_oth = jnp.where(e == 0, high, low)
    DMA = pltpu.SemaphoreType.DMA
    V = pltpu.VMEM
    rows2 = 2 * rows
    vm = pl.BlockSpec(memory_space=pltpu.VMEM)
    hb = pl.BlockSpec(memory_space=pl.ANY)
    out, grad, gg, gg_gate, gg_up, gg_down = pl.pallas_call(
        functools.partial(kernel, N, C),
        out_shape=(
            jax.ShapeDtypeStruct((rows, Dc), BF),
            jax.ShapeDtypeStruct((rows, Dc), BF),
            jax.ShapeDtypeStruct((2, 8, 128), F32),
            jax.ShapeDtypeStruct((K, Dq, W), F32),
            jax.ShapeDtypeStruct((K, Dq, W), F32),
            jax.ShapeDtypeStruct((K, W, Dq), F32),
        ),
        in_specs=[hb] * 7,
        out_specs=(vm,) * 6,
        scratch_shapes=[
            V((D, 2 * K * W), BF),
            V((K * W, D), BF),
            V((2, N, rows2, Dq), BF),
            V((2, N, rows2, Dq), BF),
            V((N, rows2, 3 * K * W), BF),
            V((2, rows, 128), F32),
            V((rows2, 2 * K * W), F32),
            V((rows2, K * W), F32),
            V((rows2, K * W), F32),
            V((2, N, rows, Dq), F32),
            V((2, N, rows, Dq), BF),
            V((2, N, rows, Dq), BF),
            V((2, N - R, rows, Dq), BF),
            V((2, N - R, rows, Dq), BF),
            V((2, 8, 128), F32),
            V((2, C, 8, 128), F32),
            V((K * W, N * rows2), BF),
            DMA((2 * K + 2,)),
            DMA((2, R)),
            DMA((2, N)),
            DMA((2, N)),
            DMA((2, N)),
            DMA((2, N)),
            DMA,
            DMA,
            DMA((2, N)),
            DMA((2, N)),
            DMA((2,)),
            DMA((2, N)),
            DMA((2, N)),
            DMA((N,)),
            DMA((N,)),
            DMA((2, N)),
            DMA((2, N)),
            DMA((2, N - R)),
            DMA((2, N - R)),
            DMA((2, C)),
            DMA((2, C)),
        ],
        compiler_params=pltpu.CompilerParams(
            collective_id=0, has_side_effects=True, vmem_limit_bytes=62 * 2**20
        ),
    )(
        tokens, cotangent, aux_own, aux_oth, w_gate, w_up, w_down.reshape(K * W, D)
    )
    mine = gg[0, :K].T
    theirs = gg[1, :K].T
    table = jnp.where(
        e == 0, jnp.concatenate([mine, theirs], 1), jnp.concatenate([theirs, mine], 1)
    )
    hot = routes[:, :, None] == jnp.arange(2 * K, dtype=jnp.int32)[None, None, :]
    gate_grad = jnp.sum(jnp.where(hot, table[:, None, :], 0.0), axis=2)
    return (out, grad, gate_grad, gg_gate, gg_up, gg_down)


def solution(mesh):
    in_specs = (
        P(("groups", "dp", "expert"), "cuts"),
        P(("groups", "dp", "expert"), None),
        P(("groups", "dp", "expert"), None),
        P("expert", None, "cuts"),
        P("expert", None, "cuts"),
        P("expert", "cuts", None),
        P(("groups", "dp", "expert"), "cuts"),
    )
    out_specs = (
        P(("groups", "dp", "expert"), "cuts"),
        P(("groups", "dp", "expert"), "cuts"),
        P(("groups", "dp", "expert"), None),
        P(("groups", "expert"), "dp", "cuts"),
        P(("groups", "expert"), "dp", "cuts"),
        P(("groups", "expert"), "cuts", "dp"),
    )
    return jax.shard_map(
        functools.partial(on_device, mesh.shape["dp"], mesh.shape["cuts"]),
        mesh=mesh, in_specs=in_specs, out_specs=out_specs, check_vma=False,
    )
```

time: 554 us -> 135 us (0.24)
  the two profiles are of different devices: /device:TPU:0 before, /device:TPU:14 now
where the time goes in v1:
time: 135 us
  Pallas kernels  123 us (91%)
  local copies, waits for them, and re-layouts  9 us (7%)
  other arithmetic  2.18 us (2%)
    pallas_call x1, Pallas kernels, on_device(): pl.pallas_call(functools.partial(kernel, N, C), out_shape=(jax.ShapeDtype...  123 us
    unnamed x15, local copies, waits for them, and re-layouts  8.16 us

profile of v1, /device:TPU:14, one launch (start us, length us, event | category | flops | bytes accessed | tf_op | source)
XLA Modules:
  0.0 135.1 jit_solution(4089420358786482559)
XLA Ops:
  0.6 0.8 select_reduce_fusion
  1.5 0.1 slice.18
  1.6 0.8 broadcast_select_fusion
  2.3 0.0 copy-start.4
  2.3 123.3 %shard_map.118 = (bf16[128,3072]{1,0:T(8,128)(2,1)}, bf16[128,3072]{1,0:T(8,128)(2,1)}, f32[2,8,128]{2,1,0:T(8,128)}, f32[2,1536,128]{2,1,0:T(8,128)}, f32[2,1536,128]{2,1,0:T(8,128)}, /*index=5*/f32[2,128,1536]{2,1,0:T(8,128)}) custom-call(bf16[128,3072]{1,0:T(8,128)(2,1)} %tok.1, bf16[128,3072]{1,0:T(8,128)(2,1)} %cot.1, ...), custom_call_target="tpu_custom_call" | custom-call | tf_op jit(solution)/shard_map/pallas_call | solution.py:319
  125.6 0.0 copy-start.3
  125.6 0.8 slice_bitcast_fusion.1
  126.4 0.0 copy-done.4
  126.4 0.6 select_reduce_fusion.1
  127.0 0.0 copy-start.2
  127.0 2.2 %copy.22 = bf16[128,3072]{1,0:T(8,128)(2,1)} copy(bf16[128,3072]{1,0:T(8,128)(2,1)} %get-tuple-element.28) | data formatting | bytes 1572864
  129.1 0.0 copy-done.3
  129.1 0.9 copy.23
  130.0 0.0 copy-done.2
  130.0 0.0 copy-start.1
  130.0 1.1 copy.24
  131.2 0.8 copy-done.1
  132.0 0.0 copy-start
  132.0 1.1 copy.25
  133.1 0.8 copy-done
  134.0 1.1 copy.26
  (2 shorter events, 0.0 us)
Async XLA Ops:
  2.3 124.0 %copy-start.4 = (s32[128,2]{0,1:T(2,128)S(1)}, s32[128,2]{0,1:T(2,128)}, u32[]{:S(2)}) copy-start(s32[128,2]{0,1:T(2,128)} %param.8) | copy-start | bytes 3076
  125.6 3.6 %copy-start.3 = (bf16[128,3072]{1,0:T(8,128)(2,1)S(1)}, bf16[128,3072]{1,0:T(8,128)(2,1)}, u32[]{:S(2)}) copy-start(bf16[128,3072]{1,0:T(8,128)(2,1)} %get-tuple-element.29) | copy-start | bytes 2359300
  127.0 3.1 %copy-start.2 = (f32[2,1536,128]{2,1,0:T(8,128)S(1)}, f32[2,1536,128]{2,1,0:T(8,128)}, u32[]{:S(2)}) copy-start(f32[2,1536,128]{2,1,0:T(8,128)} %get-tuple-element.31) | copy-start | bytes 4718596
  130.0 2.0 %copy-start.1 = (f32[2,1536,128]{2,1,0:T(8,128)S(1)}, f32[2,1536,128]{2,1,0:T(8,128)}, u32[]{:S(2)}) copy-start(f32[2,1536,128]{2,1,0:T(8,128)} %get-tuple-element.32) | copy-start | bytes 4718596
  132.0 2.0 %copy-start = (f32[2,128,1536]{2,1,0:T(8,128)S(1)}, f32[2,128,1536]{2,1,0:T(8,128)}, u32[]{:S(2)}) copy-start(f32[2,128,1536]{2,1,0:T(8,128)} %get-tuple-element.33) | copy-start | bytes 4718596

commit v2 on v1

--- a/solution.py
+++ b/solution.py
@@ -28,7 +28,7 @@
     out_o, grad_o, gg_o, g_gate, g_up, g_down,
     wgu, wd, xg, zr, hz, aux, acc, accd, hid, ploc, csend, cr, xsend, xr, ggs, ggr, hwt,
     wsem, osem, xs_s, xs_r, co_s, co_r, au_s, au_r, z_s, z_r, zl, f_s, f_r,
-    h_s, h_r, rc_s, rc_r, rx_s, rx_r, gg_s, gg_r,
+    f1_s, f1_r, xf_s, xf_r, h_s, h_r, rc_s, rc_r, rx_s, rx_r, gg_s, gg_r,
 ):
     d, e, c = lax.axis_index("dp"), lax.axis_index("expert"), lax.axis_index("cuts")
     other = 1 - e
@@ -97,19 +97,28 @@
     wd_load = pltpu.make_async_copy(wd_in, wd, wsem.at[2 * K])
     wd_load.start()
 
+    hr = rows // C
+
+    def share(slot, cc):
+        return pl.ds(pl.multiple_of(slot * rows + cc * hr, 16), hr)
+
     def z_copy(kind, p):
-        q = quarter(p)
+        part = own if kind == 0 else share(0, c)
         return rcopy(
-            xg.at[kind, p, own], zr.at[kind, d, own], z_s.at[kind, p], z_r.at[kind, d], {"dp": q}
+            xg.at[kind, p, part], zr.at[kind, d, part], z_s.at[kind, p], z_r.at[kind, d],
+            {"dp": quarter(p)},
         )
 
     def z_local(kind, p):
         return pltpu.make_async_copy(xg.at[kind, p], zr.at[kind, d], zl.at[kind])
 
+    def z_start(kind, p):
+        @pl.when(quarter(p) != d)
+        def _():
+            z_copy(kind, p).start()
+
     def arrive(kind, p):
-        if p < R:
-            loc[kind * R + p].wait()
-        else:
+        if p >= R:
             rcopy(
                 xg.at[kind, p, own], xg.at[kind, p, own], xs_s.at[kind, p], xs_r.at[kind, p],
                 {"cuts": c},
@@ -119,11 +128,7 @@
             )
             cp.start()
             c_out.append(cp)
-
-        @pl.when(quarter(p) != d)
-        def _():
-            z_copy(kind, p).start()
-
+            z_start(kind, p)
         rcopy(
             xg.at[kind, p, own], xg.at[kind, p, oth], co_s.at[kind, p], co_r.at[kind, p], core
         ).wait_recv()
@@ -134,10 +139,15 @@
 
     acc[...] = jnp.zeros_like(acc)
     accd[...] = jnp.zeros_like(accd)
-    for cp in w_loads:
-        cp.wait()
+    for kind in range(2):
+        for p in range(R):
+            loc[kind * R + p].wait()
+            z_start(kind, p)
     for p in range(N):
         arrive(0, p)
+        if p == 0:
+            for cp in w_loads:
+                cp.wait()
         acc[...] += dot(xg[0, p], wgu[cols(p), :], 1, 0)
     aux_copy.wait()
     aux_loc.wait()
@@ -223,50 +233,125 @@
             gg_out.append(cp)
     ggr[0, 0] = ggs[0]
 
-    h_out = []
-    for i in range(1, N):
-        cp = rcopy(hz.at[d], hz.at[d], h_s.at[i], h_r.at[d], {"dp": lax.rem(d + i, N)})
-        cp.start()
-        h_out.append(cp)
+    pieces = (own, oth)
+
+    def h_copy(ds, n, up):
+        at = hz.at[ds, pieces[n]]
+        to = jnp.minimum(d + 1, N - 1) if up else jnp.maximum(d - 1, 0)
+        return rcopy(at, at, h_s.at[int(up), ds, n], h_r.at[ds, n], {"dp": to})
+
+    for n in range(2):
+        @pl.when(d < N - 1)
+        def _():
+            h_copy(d, n, True).start()
+
+        @pl.when(d > 0)
+        def _():
+            h_copy(d, n, False).start()
 
     back(1)
 
     f_out = []
-    for kind in range(2):
-        for i in range(1, N):
-            ds = lax.rem(d + i, N)
-            z = zr.at[kind, ds, own]
-            rcopy(z, z, z_s.at[kind, i], z_r.at[kind, ds], {"dp": d}).wait_recv()
-            cp = rcopy(z, zr.at[kind, ds, oth], f_s.at[kind, ds], f_r.at[kind, ds], core)
-            cp.start()
-            f_out.append(cp)
     for i in range(1, N):
         ds = lax.rem(d + i, N)
-        rcopy(hz.at[ds], hz.at[ds], h_s.at[i], h_r.at[ds], {"dp": d}).wait_recv()
+        z = zr.at[0, ds, own]
+        rcopy(z, z, z_s.at[0, i], z_r.at[0, ds], {"dp": d}).wait_recv()
+        cp = rcopy(z, zr.at[0, ds, oth], f_s.at[0, ds], f_r.at[0, ds], core)
+        cp.start()
+        f_out.append(cp)
+
+    def core_copy(ds, i):
+        return rcopy(
+            zr.at[1, ds, share(0, rel(i))], zr.at[1, ds, share(1, rel(i))],
+            f1_s.at[ds, i], f1_r.at[ds, i], core,
+        )
+
+    for i in range(1, N):
+        ds = lax.rem(d + i, N)
+        z = zr.at[1, ds, share(0, c)]
+        rcopy(z, z, z_s.at[1, i], z_r.at[1, ds], {"dp": d}).wait_recv()
+        for j in range(1, C):
+            cp = rcopy(z, z, xf_s.at[ds, j], xf_r.at[ds, C - j], {"cuts": rel(j)})
+            cp.start()
+            f_out.append(cp)
+        cp = core_copy(ds, 0)
+        cp.start()
+        f_out.append(cp)
     for kind in range(2):
         z_local(kind, 0).wait()
-        for i in range(1, N):
-            ds = lax.rem(d + i, N)
-            z = zr.at[kind, ds, oth]
-            rcopy(z, z, f_s.at[kind, ds], f_r.at[kind, ds], core).wait_recv()
-
-    flat = N * 2 * rows
-    hwt[...] = hz[:, :, pl.ds(2 * K * W, K * W)].reshape(flat, K * W).T
     wt = 256 if Dq % 256 == 0 else 128
 
-    def wstep(t, _):
-        at = pl.ds(pl.multiple_of(t * wt, 128), wt)
-        full = dot(
-            zr[0, :, :, at].reshape(flat, wt), hz[:, :, pl.ds(0, 2 * K * W)].reshape(flat, 2 * K * W), 0, 0
-        )
-        down = dot(hwt[...], zr[1, :, :, at].reshape(flat, wt), 1, 0)
-        for k in range(K):
-            g_gate[k, at, :] = full[:, 2 * k * W : (2 * k + 1) * W]
-            g_up[k, at, :] = full[:, (2 * k + 1) * W : (2 * k + 2) * W]
-            g_down[k, :, at] = down[k * W : (k + 1) * W]
+    def weight_grads(ds, first):
+        hwt[...] = hz[ds, :, pl.ds(2 * K * W, K * W)].T
+
+        def wstep(t, _):
+            at = pl.ds(pl.multiple_of(t * wt, 128), wt)
+            full = dot(zr[0, ds, :, at], hz[ds, :, pl.ds(0, 2 * K * W)], 0, 0)
+            down = dot(hwt[...], zr[1, ds, :, at], 1, 0)
+            for k in range(K):
+                for ref, part in (
+                    (g_gate.at[k, at, :], full[:, 2 * k * W : (2 * k + 1) * W]),
+                    (g_up.at[k, at, :], full[:, (2 * k + 1) * W : (2 * k + 2) * W]),
+                    (g_down.at[k, :, at], down[k * W : (k + 1) * W]),
+                ):
+                    ref[...] = part if first else ref[...] + part
+            return 0
+
+        lax.fori_loop(0, Dq // wt, wstep, 0)
+
+    steps = 2 * (N - 1)
+
+    def source(t):
+        hop = t // 2 + 1
+        up = lax.rem(t, 2) == 0
+        ds = jnp.where(up, d - hop, d + hop)
+        return up, ds, (ds >= 0) & (ds < N)
+
+    def hops(t, _):
+        up, ds, there = source(t)
+
+        @pl.when(there)
+        def _():
+            for n in range(2):
+                at = hz.at[ds, pieces[n]]
+                rcopy(at, at, h_s.at[0, ds, n], h_r.at[ds, n], {"dp": d}).wait_recv()
+
+                @pl.when(up & (d < N - 1))
+                def _():
+                    h_copy(ds, n, True).start()
+
+                @pl.when(jnp.logical_not(up) & (d > 0))
+                def _():
+                    h_copy(ds, n, False).start()
+
         return 0
 
-    lax.fori_loop(0, Dq // wt, wstep, 0)
+    lax.fori_loop(0, steps, hops, 0)
+    weight_grads(d, True)
+
+    def far(t, _):
+        _, ds, there = source(t)
+
+        @pl.when(there & (t < steps))
+        def _():
+            for j in range(1, C):
+                z = zr.at[1, ds, share(0, rel(j))]
+                rcopy(z, z, xf_s.at[ds, j], xf_r.at[ds, j], {"cuts": c}).wait_recv()
+                core_copy(ds, j).start()
+
+        _, before, was = source(t - 2)
+
+        @pl.when(was & (t >= 2))
+        def _():
+            z = zr.at[0, before, oth]
+            rcopy(z, z, f_s.at[0, before], f_r.at[0, before], core).wait_recv()
+            for j in range(C):
+                core_copy(before, j).wait_recv()
+            weight_grads(before, False)
+
+        return 0
+
+    lax.fori_loop(0, steps + 2, far, 0)
 
     outs = (out_o, grad_o)
     for kind in range(2):
@@ -290,13 +375,66 @@
                 rcopy(g, g, gg_s.at[slot, i], gg_r.at[slot, i], {"cuts": c}).wait_recv()
     gg_o[...] = jnp.sum(ggr[...], axis=1)
 
-    for cp in x_out + c_out + rc_out + rx_out + gg_out + h_out + f_out:
+    for cp in x_out + c_out + rc_out + rx_out + gg_out + f_out:
         cp.wait_send()
     for kind in range(2):
         for p in range(N):
             @pl.when(quarter(p) != d)
             def _():
                 z_copy(kind, p).wait_send()
+
+    def sent(ds, _):
+        @pl.when(ds != d)
+        def _():
+            for j in range(1, C):
+                core_copy(ds, j).wait_send()
+
+        for n in range(2):
+            @pl.when((ds <= d) & (d < N - 1))
+            def _():
+                h_copy(ds, n, True).wait_send()
+
+            @pl.when((ds >= d) & (d > 0))
+            def _():
+                h_copy(ds, n, False).wait_send()
+
+        return 0
+
+    lax.fori_loop(0, N, sent, 0)
+
+
+def settle_kernel(count, *refs):
+    n = len(refs) // 3
+    sems = refs[-1]
+    loads, stores = [], []
+    for i in range(n):
+        rows = refs[i].shape[0] // count
+        for j in range(count):
+            at = pl.ds(j * rows, rows)
+            cp = pltpu.make_async_copy(refs[i].at[at], refs[2 * n + i].at[at], sems.at[0, i, j])
+            cp.start()
+            loads.append((cp, i, j, at))
+    for cp, i, j, at in loads:
+        cp.wait()
+        cp = pltpu.make_async_copy(refs[2 * n + i].at[at], refs[n + i].at[at], sems.at[1, i, j])
+        cp.start()
+        stores.append(cp)
+    for cp in stores:
+        cp.wait()
+
+
+def settle(*arrays):
+    n = len(arrays)
+    hb = pl.BlockSpec(memory_space=pl.ANY)
+    return pl.pallas_call(
+        functools.partial(settle_kernel, 2),
+        out_shape=tuple(jax.ShapeDtypeStruct(a.shape, a.dtype) for a in arrays),
+        in_specs=[hb] * n,
+        out_specs=(hb,) * n,
+        scratch_shapes=[pltpu.VMEM(a.shape, a.dtype) for a in arrays]
+        + [pltpu.SemaphoreType.DMA((2, n, 2))],
+        compiler_params=pltpu.CompilerParams(vmem_limit_bytes=62 * 2**20),
+    )(*arrays)
 
 
 def on_device(N, C, tokens, routes, gates, w_gate, w_up, w_down, cotangent):
@@ -345,7 +483,7 @@
             V((2, N - R, rows, Dq), BF),
             V((2, 8, 128), F32),
             V((2, C, 8, 128), F32),
-            V((K * W, N * rows2), BF),
+            V((K * W, rows2), BF),
             DMA((2 * K + 2,)),
             DMA((2, R)),
             DMA((2, N)),
@@ -359,8 +497,12 @@
             DMA((2,)),
             DMA((2, N)),
             DMA((2, N)),
-            DMA((N,)),
-            DMA((N,)),
+            DMA((N, C)),
+            DMA((N, C)),
+            DMA((N, C)),
+            DMA((N, C)),
+            DMA((2, N, 2)),
+            DMA((N, 2)),
             DMA((2, N)),
             DMA((2, N)),
             DMA((2, N - R)),
@@ -374,6 +516,7 @@
     )(
         tokens, cotangent, aux_own, aux_oth, w_gate, w_up, w_down.reshape(K * W, D)
     )
+    out, grad, gg_gate, gg_up, gg_down = settle(out, grad, gg_gate, gg_up, gg_down)
     mine = gg[0, :K].T
     theirs = gg[1, :K].T
     table = jnp.where(

time: 135 us -> 112 us (0.83)
  the two profiles are of different devices: /device:TPU:14 before, /device:TPU:0 now
where the time goes in v2:
time: 112 us; the launch traced here: 111 us
  Pallas kernels  108 us (96%)
  other arithmetic  2.18 us (2%)
    pallas_call x1, Pallas kernels, on_device(): pl.pallas_call(functools.partial(kernel, N, C), out_shape=(jax.ShapeDtype...  103 us
    pallas_call x1, Pallas kernels, settle(): pl.pallas_call(functools.partial(settle_kernel, 2), out_shape=tuple((jax....  5.27 us

profile of v2, /device:TPU:0, one launch (start us, length us, event | category | flops | bytes accessed | tf_op | source)
XLA Modules:
  0.0 111.5 jit_solution(467864662046038072)
XLA Ops:
  0.6 0.8 select_reduce_fusion
  1.5 0.1 slice.18
  1.6 0.8 broadcast_select_fusion
  2.3 0.0 copy-start
  2.3 102.6 %shard_map.118 = (bf16[128,3072]{1,0:T(8,128)(2,1)}, bf16[128,3072]{1,0:T(8,128)(2,1)}, f32[2,8,128]{2,1,0:T(8,128)}, f32[2,1536,128]{2,1,0:T(8,128)}, f32[2,1536,128]{2,1,0:T(8,128)}, /*index=5*/f32[2,128,1536]{2,1,0:T(8,128)}) custom-call(bf16[128,3072]{1,0:T(8,128)(2,1)} %tok.1, bf16[128,3072]{1,0:T(8,128)(2,1)} %cot.1, ...), custom_call_target="tpu_custom_call" | custom-call | tf_op jit(solution)/shard_map/pallas_call | solution.py:457
  104.9 0.7 slice_bitcast_fusion.1
  105.6 0.0 copy-done
  105.6 0.6 select_reduce_fusion.1
  106.2 5.3 %shard_map.119 = (bf16[128,3072]{1,0:T(8,128)(2,1)}, bf16[128,3072]{1,0:T(8,128)(2,1)}, f32[2,1536,128]{2,1,0:T(8,128)}, f32[2,1536,128]{2,1,0:T(8,128)}, f32[2,128,1536]{2,1,0:T(8,128)}) custom-call(bf16[128,3072]{1,0:T(8,128)(2,1)} %get-tuple-element.17.refs_0_, bf16[128,3072]{1,0:T(8,128)(2,1)} %get-tuple-element.18.refs_1_, ...), custom_call_target="tpu_custom_call" | custom-call | tf_op jit(solution)/shard_map/pallas_call | solution.py:429
  (2 shorter events, 0.0 us)
Async XLA Ops:
  2.3 103.3 %copy-start = (s32[128,2]{0,1:T(2,128)S(1)}, s32[128,2]{0,1:T(2,128)}, u32[]{:S(2)}) copy-start(s32[128,2]{0,1:T(2,128)} %param.8) | copy-start | bytes 3076

commit v3 on v2

--- a/solution.py
+++ b/solution.py
@@ -24,9 +24,9 @@
 
 
 def kernel(
-    N, C, tok, cot, aux_own, aux_oth, wg, wu, wd_in,
-    out_o, grad_o, gg_o, g_gate, g_up, g_down,
-    wgu, wd, xg, zr, hz, aux, acc, accd, hid, ploc, csend, cr, xsend, xr, ggs, ggr, hwt,
+    N, C, tok, cot, routes, gates, wg, wu, wd_in,
+    out_o, grad_o, gate_o, g_gate, g_up, g_down,
+    wgu, wd, xg, zr, hz, aux, auxs, acc, accd, hid, ploc, csend, cr, xsend, xr, ggs, ggr, hwt,
     wsem, osem, xs_s, xs_r, co_s, co_r, au_s, au_r, z_s, z_r, zl, f_s, f_r,
     f1_s, f1_r, xf_s, xf_r, h_s, h_r, rc_s, rc_r, rx_s, rx_r, gg_s, gg_r,
 ):
@@ -68,10 +68,6 @@
     x_out = []
     c_out = []
     loc = []
-    aux_copy = rcopy(aux_oth, aux.at[1], au_s, au_r, core)
-    aux_copy.start()
-    aux_loc = pltpu.make_async_copy(aux_own, aux.at[0], wsem.at[2 * K + 1])
-    aux_loc.start()
     for kind in range(2):
         for r in range(R):
             src = ins[kind].at[:, pl.ds(r * Dq, Dq)]
@@ -108,6 +104,20 @@
             xg.at[kind, p, part], zr.at[kind, d, part], z_s.at[kind, p], z_r.at[kind, d],
             {"dp": quarter(p)},
         )
+
+    def dense(index):
+        ids = lax.broadcasted_iota(jnp.int32, (8, rows), 0)
+        want = ids + index * K
+        table = jnp.zeros((8, rows), F32)
+        for j in range(2):
+            hit = (routes[j : j + 1, :] == want) & (ids < K)
+            table = table + jnp.where(hit, gates[j : j + 1, :], 0.0)
+        return table
+
+    aux[0] = dense(e)
+    auxs[...] = dense(other)
+    aux_copy = rcopy(auxs, aux.at[1], au_s, au_r, core)
+    aux_copy.start()
 
     def z_local(kind, p):
         return pltpu.make_async_copy(xg.at[kind, p], zr.at[kind, d], zl.at[kind])
@@ -150,11 +160,11 @@
                 cp.wait()
         acc[...] += dot(xg[0, p], wgu[cols(p), :], 1, 0)
     aux_copy.wait()
-    aux_loc.wait()
+    by_token = [jnp.concatenate([aux[n], jnp.zeros((120, rows), F32)], 0).T for n in range(2)]
     wd_load.wait()
 
     def weight(k):
-        return jnp.concatenate([aux[0, :, k : k + 1], aux[1, :, k : k + 1]], axis=0)
+        return jnp.concatenate([t[:, k : k + 1] for t in by_token], axis=0)
 
     for k in range(K):
         gs = pl.ds(2 * k * W, W)
@@ -326,35 +336,8 @@
 
         return 0
 
-    lax.fori_loop(0, steps, hops, 0)
-    weight_grads(d, True)
-
-    def far(t, _):
-        _, ds, there = source(t)
-
-        @pl.when(there & (t < steps))
-        def _():
-            for j in range(1, C):
-                z = zr.at[1, ds, share(0, rel(j))]
-                rcopy(z, z, xf_s.at[ds, j], xf_r.at[ds, j], {"cuts": c}).wait_recv()
-                core_copy(ds, j).start()
-
-        _, before, was = source(t - 2)
-
-        @pl.when(was & (t >= 2))
-        def _():
-            z = zr.at[0, before, oth]
-            rcopy(z, z, f_s.at[0, before], f_r.at[0, before], core).wait_recv()
-            for j in range(C):
-                core_copy(before, j).wait_recv()
-            weight_grads(before, False)
-
-        return 0
-
-    lax.fori_loop(0, steps + 2, far, 0)
-
     outs = (out_o, grad_o)
-    for kind in range(2):
+    def final(kind):
         for r in range(R):
             rcopy(
                 csend.at[kind, r], cr.at[kind, r], rc_s.at[kind, r], rc_r.at[kind, r], core
@@ -368,12 +351,49 @@
                 total = total + xr[kind, n].astype(F32)
             outs[kind][:, pl.ds(r * Dq, Dq)] = total.astype(BF)
 
+    lax.fori_loop(0, steps, hops, 0)
+    final(0)
+    weight_grads(d, True)
+
+    def far(t, _):
+        _, ds, there = source(t)
+
+        @pl.when(there & (t < steps))
+        def _():
+            for j in range(1, C):
+                z = zr.at[1, ds, share(0, rel(j))]
+                rcopy(z, z, xf_s.at[ds, j], xf_r.at[ds, j], {"cuts": c}).wait_recv()
+                core_copy(ds, j).start()
+
+        _, before, was = source(t - 2)
+
+        @pl.when(was & (t >= 2))
+        def _():
+            z = zr.at[0, before, oth]
+            rcopy(z, z, f_s.at[0, before], f_r.at[0, before], core).wait_recv()
+            for j in range(C):
+                core_copy(before, j).wait_recv()
+            weight_grads(before, False)
+
+        return 0
+
+    lax.fori_loop(0, steps + 2, far, 0)
+
+    final(1)
+
     for i in range(C):
         for slot in range(2):
             if i or slot:
                 g = ggr.at[slot, i]
                 rcopy(g, g, gg_s.at[slot, i], gg_r.at[slot, i], {"cuts": c}).wait_recv()
-    gg_o[...] = jnp.sum(ggr[...], axis=1)
+    sums = jnp.sum(ggr[...], axis=1)
+    for j in range(2):
+        total = jnp.zeros((1, rows), F32)
+        for n, index in enumerate((e, other)):
+            for k in range(K):
+                hit = routes[j : j + 1, :] == index * K + k
+                total = total + jnp.where(hit, sums[n, k : k + 1, :], 0.0)
+        gate_o[j : j + 1, :] = total
 
     for cp in x_out + c_out + rc_out + rx_out + gg_out + f_out:
         cp.wait_send()
@@ -408,8 +428,9 @@
     sems = refs[-1]
     loads, stores = [], []
     for i in range(n):
-        rows = refs[i].shape[0] // count
-        for j in range(count):
+        parts = 1 if refs[i].shape[0] % count or len(refs[i].shape) == 2 and refs[i].shape[0] < 32 else count
+        rows = refs[i].shape[0] // parts
+        for j in range(parts):
             at = pl.ds(j * rows, rows)
             cp = pltpu.make_async_copy(refs[i].at[at], refs[2 * n + i].at[at], sems.at[0, i, j])
             cp.start()
@@ -442,29 +463,22 @@
     rows, Dc = tokens.shape
     R = N // C
     Dq = Dc // R
-    e = lax.axis_index("expert")
-    lanes = jnp.arange(128, dtype=jnp.int32)
-    onehot = (routes[:, :, None] == lanes[None, None, :]) & (lanes < 2 * K)[None, None, :]
-    dense = jnp.sum(jnp.where(onehot, gates[:, :, None], 0.0), axis=1)
-    low, high = dense, jnp.roll(dense, -K, axis=1)
-    aux_own = jnp.where(e == 0, low, high)
-    aux_oth = jnp.where(e == 0, high, low)
     DMA = pltpu.SemaphoreType.DMA
     V = pltpu.VMEM
     rows2 = 2 * rows
     vm = pl.BlockSpec(memory_space=pltpu.VMEM)
     hb = pl.BlockSpec(memory_space=pl.ANY)
-    out, grad, gg, gg_gate, gg_up, gg_down = pl.pallas_call(
+    results = pl.pallas_call(
         functools.partial(kernel, N, C),
         out_shape=(
             jax.ShapeDtypeStruct((rows, Dc), BF),
             jax.ShapeDtypeStruct((rows, Dc), BF),
-            jax.ShapeDtypeStruct((2, 8, 128), F32),
+            jax.ShapeDtypeStruct((2, rows), F32),
             jax.ShapeDtypeStruct((K, Dq, W), F32),
             jax.ShapeDtypeStruct((K, Dq, W), F32),
             jax.ShapeDtypeStruct((K, W, Dq), F32),
         ),
-        in_specs=[hb] * 7,
+        in_specs=[hb, hb, vm, vm, hb, hb, hb],
         out_specs=(vm,) * 6,
         scratch_shapes=[
             V((D, 2 * K * W), BF),
@@ -472,7 +486,8 @@
             V((2, N, rows2, Dq), BF),
             V((2, N, rows2, Dq), BF),
             V((N, rows2, 3 * K * W), BF),
-            V((2, rows, 128), F32),
+            V((2, 8, rows), F32),
+            V((8, rows), F32),
             V((rows2, 2 * K * W), F32),
             V((rows2, K * W), F32),
             V((rows2, K * W), F32),
@@ -514,17 +529,10 @@
             collective_id=0, has_side_effects=True, vmem_limit_bytes=62 * 2**20
         ),
     )(
-        tokens, cotangent, aux_own, aux_oth, w_gate, w_up, w_down.reshape(K * W, D)
+        tokens, cotangent, routes.T, gates.T, w_gate, w_up, w_down.reshape(K * W, D)
     )
-    out, grad, gg_gate, gg_up, gg_down = settle(out, grad, gg_gate, gg_up, gg_down)
-    mine = gg[0, :K].T
-    theirs = gg[1, :K].T
-    table = jnp.where(
-        e == 0, jnp.concatenate([mine, theirs], 1), jnp.concatenate([theirs, mine], 1)
-    )
-    hot = routes[:, :, None] == jnp.arange(2 * K, dtype=jnp.int32)[None, None, :]
-    gate_grad = jnp.sum(jnp.where(hot, table[:, None, :], 0.0), axis=2)
-    return (out, grad, gate_grad, gg_gate, gg_up, gg_down)
+    out, grad, gate_grad, gg_gate, gg_up, gg_down = settle(*results)
+    return (out, grad, gate_grad.T, gg_gate, gg_up, gg_down)
 
 
 def solution(mesh):

time: 112 us -> 110 us (0.982)
  other arithmetic: 2.18 us -> 0 us
    reduce_sum x2 -> x0, other arithmetic: 1.42 us -> none  [the longest x1 0.83 us: on_device(): dense = jnp.sum(jnp.where(onehot, gates[:, :, None], 0.0), axis=1)]
where the time goes in v3:
time: 110 us; the launch traced here: 109 us
  Pallas kernels  109 us (99%)
    pallas_call x1, Pallas kernels, on_device(): pl.pallas_call(functools.partial(kernel, N, C), out_shape=(jax.ShapeDtype...  103 us
    pallas_call x1, Pallas kernels, settle(): pl.pallas_call(functools.partial(settle_kernel, 2), out_shape=tuple((jax....  5.31 us

profile of v3, /device:TPU:0, one launch (start us, length us, event | category | flops | bytes accessed | tf_op | source)
XLA Modules:
  0.0 109.3 jit_solution(2530228790505678820)
XLA Ops:
  0.6 103.3 %shard_map.118 = (bf16[128,3072]{1,0:T(8,128)(2,1)}, bf16[128,3072]{1,0:T(8,128)(2,1)}, f32[2,128]{1,0:T(2,128)}, f32[2,1536,128]{2,1,0:T(8,128)}, f32[2,1536,128]{2,1,0:T(8,128)}, /*index=5*/f32[2,128,1536]{2,1,0:T(8,128)}) custom-call(bf16[128,3072]{1,0:T(8,128)(2,1)} %tok.1, bf16[128,3072]{1,0:T(8,128)(2,1)} %cot.1, s32[2,128]{1,0:T(2,128)} %bitcast.5, ...), custom_call_target="tpu_custom_call" | custom-call | tf_op jit(solution)/shard_map/pallas_call | solution.py:471
  103.9 5.3 %shard_map.119 = (bf16[128,3072]{1,0:T(8,128)(2,1)}, bf16[128,3072]{1,0:T(8,128)(2,1)}, f32[2,128]{1,0:T(2,128)}, f32[2,1536,128]{2,1,0:T(8,128)}, f32[2,1536,128]{2,1,0:T(8,128)}, /*index=5*/f32[2,128,1536]{2,1,0:T(8,128)}) custom-call(bf16[128,3072]{1,0:T(8,128)(2,1)} %get-tuple-element.18.refs_0_, bf16[128,3072]{1,0:T(8,128)(2,1)} %get-tuple-element.19.refs_1_, ...), custom_call_target="tpu_custom_call" | custom-call | tf_op jit(solution)/shard_map/pallas_call | solution.py:450

commit v4 on v3

--- a/solution.py
+++ b/solution.py
@@ -99,7 +99,7 @@
         return pl.ds(pl.multiple_of(slot * rows + cc * hr, 16), hr)
 
     def z_copy(kind, p):
-        part = own if kind == 0 else share(0, c)
+        part = share(0, c) if kind == 0 else own
         return rcopy(
             xg.at[kind, p, part], zr.at[kind, d, part], z_s.at[kind, p], z_r.at[kind, d],
             {"dp": quarter(p)},
@@ -259,27 +259,18 @@
         def _():
             h_copy(d, n, False).start()
 
-    back(1)
-
     f_out = []
+
+    def core_copy(ds, i):
+        return rcopy(
+            zr.at[0, ds, share(0, rel(i))], zr.at[0, ds, share(1, rel(i))],
+            f1_s.at[ds, i], f1_r.at[ds, i], core,
+        )
+
     for i in range(1, N):
         ds = lax.rem(d + i, N)
-        z = zr.at[0, ds, own]
+        z = zr.at[0, ds, share(0, c)]
         rcopy(z, z, z_s.at[0, i], z_r.at[0, ds], {"dp": d}).wait_recv()
-        cp = rcopy(z, zr.at[0, ds, oth], f_s.at[0, ds], f_r.at[0, ds], core)
-        cp.start()
-        f_out.append(cp)
-
-    def core_copy(ds, i):
-        return rcopy(
-            zr.at[1, ds, share(0, rel(i))], zr.at[1, ds, share(1, rel(i))],
-            f1_s.at[ds, i], f1_r.at[ds, i], core,
-        )
-
-    for i in range(1, N):
-        ds = lax.rem(d + i, N)
-        z = zr.at[1, ds, share(0, c)]
-        rcopy(z, z, z_s.at[1, i], z_r.at[1, ds], {"dp": d}).wait_recv()
         for j in range(1, C):
             cp = rcopy(z, z, xf_s.at[ds, j], xf_r.at[ds, C - j], {"cuts": rel(j)})
             cp.start()
@@ -287,6 +278,22 @@
         cp = core_copy(ds, 0)
         cp.start()
         f_out.append(cp)
+
+    back(1)
+
+    for i in range(1, N):
+        ds = lax.rem(d + i, N)
+        z = zr.at[1, ds, own]
+        rcopy(z, z, z_s.at[1, i], z_r.at[1, ds], {"dp": d}).wait_recv()
+        cp = rcopy(z, zr.at[1, ds, oth], f_s.at[1, ds], f_r.at[1, ds], core)
+        cp.start()
+        f_out.append(cp)
+    for i in range(1, N):
+        ds = lax.rem(d + i, N)
+        for j in range(1, C):
+            z = zr.at[0, ds, share(0, rel(j))]
+            rcopy(z, z, xf_s.at[ds, j], xf_r.at[ds, j], {"cuts": c}).wait_recv()
+            core_copy(ds, j).start()
     for kind in range(2):
         z_local(kind, 0).wait()
     wt = 256 if Dq % 256 == 0 else 128
@@ -333,6 +340,12 @@
                 @pl.when(jnp.logical_not(up) & (d > 0))
                 def _():
                     h_copy(ds, n, False).start()
+
+            z = zr.at[1, ds, oth]
+            rcopy(z, z, f_s.at[1, ds], f_r.at[1, ds], core).wait_recv()
+            for j in range(C):
+                core_copy(ds, j).wait_recv()
+            weight_grads(ds, False)
 
         return 0
 
@@ -351,33 +364,9 @@
                 total = total + xr[kind, n].astype(F32)
             outs[kind][:, pl.ds(r * Dq, Dq)] = total.astype(BF)
 
+    weight_grads(d, True)
+    final(0)
     lax.fori_loop(0, steps, hops, 0)
-    final(0)
-    weight_grads(d, True)
-
-    def far(t, _):
-        _, ds, there = source(t)
-
-        @pl.when(there & (t < steps))
-        def _():
-            for j in range(1, C):
-                z = zr.at[1, ds, share(0, rel(j))]
-                rcopy(z, z, xf_s.at[ds, j], xf_r.at[ds, j], {"cuts": c}).wait_recv()
-                core_copy(ds, j).start()
-
-        _, before, was = source(t - 2)
-
-        @pl.when(was & (t >= 2))
-        def _():
-            z = zr.at[0, before, oth]
-            rcopy(z, z, f_s.at[0, before], f_r.at[0, before], core).wait_recv()
-            for j in range(C):
-                core_copy(before, j).wait_recv()
-            weight_grads(before, False)
-
-        return 0
-
-    lax.fori_loop(0, steps + 2, far, 0)
 
     final(1)
 

time: 110 us -> 107 us (0.973)
  Pallas kernels: 109 us -> 106 us
    pallas_call x1, Pallas kernels: 103 us -> 101 us  [on_device(): pl.pallas_call(functools.partial(kernel, N, C), out_shape=(jax.ShapeDtype...]
where the time goes in v4:
time: 107 us
  Pallas kernels  106 us (99%)
    pallas_call x1, Pallas kernels, on_device(): pl.pallas_call(functools.partial(kernel, N, C), out_shape=(jax.ShapeDtype...  101 us
    pallas_call x1, Pallas kernels, settle(): pl.pallas_call(functools.partial(settle_kernel, 2), out_shape=tuple((jax....  5.31 us

profile of v4, /device:TPU:0, one launch (start us, length us, event | category | flops | bytes accessed | tf_op | source)
XLA Modules:
  0.0 107.1 jit_solution(2702045220536936875)
XLA Ops:
  0.6 101.1 %shard_map.118 = (bf16[128,3072]{1,0:T(8,128)(2,1)}, bf16[128,3072]{1,0:T(8,128)(2,1)}, f32[2,128]{1,0:T(2,128)}, f32[2,1536,128]{2,1,0:T(8,128)}, f32[2,1536,128]{2,1,0:T(8,128)}, /*index=5*/f32[2,128,1536]{2,1,0:T(8,128)}) custom-call(bf16[128,3072]{1,0:T(8,128)(2,1)} %tok.1, bf16[128,3072]{1,0:T(8,128)(2,1)} %cot.1, s32[2,128]{1,0:T(2,128)} %bitcast.5, ...), custom_call_target="tpu_custom_call" | custom-call | tf_op jit(solution)/shard_map/pallas_call | solution.py:460
  101.8 5.3 %shard_map.119 = (bf16[128,3072]{1,0:T(8,128)(2,1)}, bf16[128,3072]{1,0:T(8,128)(2,1)}, f32[2,128]{1,0:T(2,128)}, f32[2,1536,128]{2,1,0:T(8,128)}, f32[2,1536,128]{2,1,0:T(8,128)}, /*index=5*/f32[2,128,1536]{2,1,0:T(8,128)}) custom-call(bf16[128,3072]{1,0:T(8,128)(2,1)} %get-tuple-element.18.refs_0_, bf16[128,3072]{1,0:T(8,128)(2,1)} %get-tuple-element.19.refs_1_, ...), custom_call_target="tpu_custom_call" | custom-call | tf_op jit(solution)/shard_map/pallas_call | solution.py:439
